TPU v7x, 32 devices: a whole 2x2x4 slice. The times are simulated.
32 devices in a mesh: groups: 2 (over y), blk: 4 (over z), proj: 2 (over x), rep: 2 (over core).
Axes of the slice: x: 2, y: 2, z: 4, core: 2. Of those that a mesh axis runs over, the one named last changes fastest.
Arguments:
- activations: bfloat16 [36864, 4096], P(('groups', 'blk', 'rep'), 'proj'), parts along dimension 0, may hold values from -6 to 6
- out_grads: bfloat16 [36864, 4096], P(('groups', 'blk', 'rep'), 'proj'), parts along dimension 0, may hold values from -6 to 6
- in_proj: bfloat16 [4096, 64], P('proj'), may hold values from -0.09375 to 0.09375
- out_proj: bfloat16 [4096, 64], P('proj'), may hold values from -0.09375 to 0.09375
- precond_queries: bfloat16 [128, 4096], P(('blk', 'rep'), 'proj'), may hold values from -0.03125 to 0.03125
- counts: int32 [16, 256], P(('groups', 'blk', 'rep')), parts along dimension 0, may hold values from 1 to 576, 2304 in all within a row
- owners: int32 [16, 256], P(('groups', 'blk', 'rep')), parts along dimension 0, may hold values from 0 to 3, as said below
Outputs:
- scores: float32 [128, 4096], P('proj', ('groups', 'blk', 'rep')), parts along dimension 1
There are 2 independent parts, one for each index of `groups`. A program takes and returns all parts, laid end to end along the dimension named above; an argument that names none is the same for every part. Nothing has to cross between parts.
Inputs may be any that keep to these rules, and one draw needn't show every extreme that they name: Each row lists the counts of one shard's documents in order; a row sums to 2304, and its largest count is 576. `owners`: no owner is named by more than 64 documents of one shard; one owner is named by exactly 64 documents of every shard.
All inputs are finite; a program needn't handle non-finite values.
Results may differ from a plain program's by a relative error of at most 0.0041.
Values may be sent and summed in bfloat16 or wider, within the bound.
A program may use at most 128 MiB of HBM per device.

v0:
```python
import jax
import jax.numpy as jnp
from jax import lax
from jax.sharding import PartitionSpec as P

CAP = 64


def score_block(queries, doc_rows):
    partial_value = lax.dot_general(
        lax.all_gather(queries, ("blk", "rep"), axis=0, tiled=True),
        doc_rows,
        (((1,), (1,)), ((), ())),
        preferred_element_type=jnp.float32,
    )
    return lax.psum_scatter(partial_value, "proj", scatter_dimension=0, tiled=True)


def per_device(activations, out_grads, in_proj, out_proj, precond_queries, counts, owners):
    input_part = jnp.dot(activations, in_proj, preferred_element_type=jnp.float32)
    output_part = jnp.dot(out_grads, out_proj, preferred_element_type=jnp.float32)
    in_factor, out_factor = lax.psum((input_part, output_part), "proj")
    slice_width = in_factor.shape[1] // lax.axis_size("proj")
    input_local = lax.dynamic_slice_in_dim(
        in_factor, lax.axis_index("proj") * slice_width, slice_width, 1
    )
    tokens_here = activations.shape[0]
    token_grads = (
        (input_local[:, :, None] * out_factor[:, None, :])
        .reshape(tokens_here, -1)
        .astype(jnp.bfloat16)
    )
    lengths = counts[0]
    doc_ends = jnp.cumsum(lengths)
    starts = doc_ends - lengths
    position = jnp.arange(tokens_here, dtype=jnp.int32)
    member = (
        (position[None, :] >= starts[:, None]) & (position[None, :] < doc_ends[:, None])
    ).astype(jnp.bfloat16)
    doc_grads = jnp.dot(member, token_grads, preferred_element_type=jnp.float32).astype(
        jnp.bfloat16
    )
    owner_count = lax.axis_size("blk")
    targets = owners[0]
    onehot = (targets[:, None] == jnp.arange(owner_count, dtype=jnp.int32)[None, :]).astype(
        jnp.int32
    )
    earlier = jnp.cumsum(onehot, axis=0) - onehot
    slot_rank = jnp.sum(earlier * onehot, axis=1)
    capacity = CAP
    slot_index = targets * capacity + slot_rank
    local_scores = score_block(precond_queries, doc_grads)
    outgoing = (
        jnp.zeros((local_scores.shape[0], owner_count * capacity), jnp.float32)
        .at[:, slot_index]
        .set(local_scores)
    )
    return lax.all_to_all(outgoing, "blk", split_axis=1, concat_axis=1, tiled=True)


def solution(mesh):
    placed = (
        P(("groups", "blk", "rep"), "proj"),
        P(("groups", "blk", "rep"), "proj"),
        P("proj", None),
        P("proj", None),
        P(("blk", "rep"), "proj"),
        P(("groups", "blk", "rep"), None),
        P(("groups", "blk", "rep"), None),
    )
    return jax.shard_map(
        per_device,
        mesh=mesh,
        in_specs=placed,
        out_specs=P("proj", ("groups", "blk", "rep")),
        check_vma=False,
    )
```

profile of v0, /device:TPU:0, one launch (start us, length us, event | category | flops | bytes accessed | tf_op | source)
XLA Modules:
  0.0 111.9 jit_solution(9951212970262849736)
XLA Ops:
  6.5 0.9 copy-done
  7.5 7.6 %fusion.13 = f32[2304,64]{0,1:T(8,128)} fusion(bf16[2304,2048]{1,0:T(8,128)(2,1)} %param.7, bf16[2048,64]{0,1:T(8,128)(2,1)S(1)} %copy-done), kind=kOutput, calls=%fused_computation.25 | convolution fusion | flops 603979776 | bytes 10289152 | tf_op jit(solution)/shard_map/dot_general | solution.py:20
  15.2 3.8 %fusion.14 = f32[2304,64]{0,1:T(8,128)} fusion(bf16[2304,2048]{1,0:T(8,128)(2,1)S(1)} %copy-done.1, bf16[2048,64]{0,1:T(8,128)(2,1)S(1)} %copy-done.2), kind=kOutput, calls=%fused_computation.26 | convolution fusion | flops 603979776 | bytes 10289152 | tf_op jit(solution)/shard_map/dot_general | solution.py:21
  19.0 0.3 reduce-window.19
  19.5 1.2 %reduce-window.15 = s32[4,2,128]{2,1,0:T(2,128)S(1)} reduce-window(s32[4,2,128]{2,1,0:T(2,128)S(1)} %compare_convert_fusion, s32[]{:T(128)} %constant.10.clone.1), window={size=1x1x128 pad=0_0x0_0x127_0}, to_apply=%region_0.0 | reduce-window | flops 130048 | bytes 8196 | tf_op jit(solution)/shard_map/reduce-window
  20.7 0.1 slice.17
  20.8 0.1 copy.16
  20.9 0.1 copy.17
  21.0 0.1 slice_reduce_fusion
  21.3 16.5 %all_gather.3 = bf16[128,2048]{1,0:T(8,128)(2,1)S(1)} all-gather(bf16[16,2048]{1,0:T(8,128)(2,1)S(1)} %copy-done.3), channel_id=1, replica_groups=mesh['groups'=2,'blk'=4,'proj'=2,'rep'=2] {'blk','rep'}, dimensions={0}, use_global_device_ids=true | all-gather | bytes 589824 | tf_op jit(solution)/shard_map/all_gather | solution.py:11
  37.8 27.2 %all-reduce.3.cloned.1.call-done = (f32[2304,64]{0,1:T(8,128)}, f32[2304,64]{0,1:T(8,128)}) async-done(((f32[2304,64]{0,1:T(8,128)}, f32[2304,64]{0,1:T(8,128)}), (f32[2304,64]{0,1:T(8,128)}, f32[2304,64]{0,1:T(8,128)})) %all-reduce.3.cloned.1.call-update) | async-done | bytes 1179664 | tf_op jit(solution)/shard_map/psum | solution.py:22
  64.9 1.0 constant_dynamic-slice_fusion
  65.9 7.4 %multiply_convert_fusion = bf16[2304,32,64]{0,2,1:T(8,128)(2,1)} fusion(f32[2304,64]{0,1:T(8,128)} %get-tuple-element.5, f32[2304,32]{0,1:T(8,128)S(1)} %constant_dynamic-slice_fusion), kind=kLoop, calls=%fused_computation.1 | loop fusion | flops 9437184 | bytes 10321920 | tf_op jit(solution)/shard_map/convert_element_type | solution.py:31
  73.3 6.0 %convolution_bitcast_fusion = f32[128,256]{0,1:T(8,128)S(1)} fusion(bf16[128,2048]{1,0:T(8,128)(2,1)S(1)} %all_gather.3, bf16[2304,2048]{0,1:T(8,128)(2,1)} %bitcast.49, s32[256]{0:T(256)S(1)} %get-tuple-element.8, s32[256]{0:T(256)S(1)} %get-tuple-element.7), kind=kOutput, calls=%fused_computation.8 | convolution fusion | flops 2552430592 | bytes 10094592 | tf_op jit(solution)/shard_map/dot_general | solution.py:10
  79.3 0.7 copy.20
  80.1 10.4 %reduce-scatter.4.cloned.1.call-done = f32[64,256]{1,0:T(8,128)} async-done(((f32[128,256]{1,0:T(8,128)}), f32[64,256]{1,0:T(8,128)}) %reduce-scatter.4.cloned.1.call-update) | async-done | bytes 65552
  90.4 0.9 copy.21
  91.4 1.2 %scatter_custom_fusion = f32[64,256]{0,1:T(8,128)S(1)} fusion(s32[256]{0:T(256)S(1)} %bitcast.58, f32[64,256]{0,1:T(8,128)S(1)} %copy.21, f32[]{:T(128)} %constant.7.clone.1), kind=kCustom, calls=%fused_computation.9 | custom fusion | bytes 196612 | tf_op jit(solution)/shard_map/scatter | solution.py:56
  92.6 0.1 reshape.108
  92.7 10.1 %all_to_all.12 = f32[4,1,4096]{2,1,0:T(1,128)S(1)} all-to-all(f32[4,1,4096]{2,1,0:T(1,128)S(1)} %reshape.108), channel_id=1, replica_groups=mesh['groups'=2,'blk'=4,'proj'=2,'rep'=2] {'blk'}, dimensions={0} | all-to-all | bytes 131072 | tf_op jit(solution)/shard_map/all_to_all | solution.py:58
  102.9 0.5 broadcast.55
  103.4 0.8 reduce.2
  104.2 0.1 reshape.109
  104.3 0.7 copy.19
  (24 shorter events, 0.4 us)
Async XLA Ops:
  6.5 1.0 copy-start
  6.5 8.6 %copy-start.2 = (bf16[2048,64]{0,1:T(8,128)(2,1)S(1)}, bf16[2048,64]{0,1:T(8,128)(2,1)}, u32[]{:S(2)}) copy-start(bf16[2048,64]{0,1:T(8,128)(2,1)} %param.10) | copy-start | bytes 786436
  6.5 58.4 %all-reduce.3.cloned.1.call-start = ((), (), s32[]{:S(2)}) async-start(), calls=%async_computation.3 | async-start | bytes 2359296 | tf_op jit(solution)/shard_map/psum | solution.py:22
  7.5 7.7 %copy-start.1 = (bf16[2304,2048]{1,0:T(8,128)(2,1)S(1)}, bf16[2304,2048]{1,0:T(8,128)(2,1)}, u32[]{:S(2)}) copy-start(bf16[2304,2048]{1,0:T(8,128)(2,1)} %param.8) | copy-start | bytes 28311556
  15.1 3.9 %copy-start.5 = (s32[1,256]{1,0:T(1,128)S(1)}, s32[1,256]{1,0:T(1,128)}, u32[]{:S(2)}) copy-start(s32[1,256]{1,0:T(1,128)} %param.12) | copy-start | bytes 3076
  15.1 4.3 %copy-start.4 = (s32[1,256]{1,0:T(1,128)S(1)}, s32[1,256]{1,0:T(1,128)}, u32[]{:S(2)}) copy-start(s32[1,256]{1,0:T(1,128)} %param.13) | copy-start | bytes 3076
  15.2 6.1 %copy-start.3 = (bf16[16,2048]{1,0:T(8,128)(2,1)S(1)}, bf16[16,2048]{1,0:T(8,128)(2,1)}, u32[]{:S(2)}) copy-start(bf16[16,2048]{1,0:T(8,128)(2,1)} %param.11) | copy-start | bytes 196612
  19.0 71.5 %reduce-scatter.4.cloned.1.call-start = ((), (), s32[]{:S(2)}) async-start(), calls=%async_computation.2 | async-start | bytes 196608
Sparse Core Ops, SparseCore 0:
  19.1 45.7 all-reduce.2
  80.1 10.2 reduce-scatter.3
where the time goes:
time: 112 us
  waiting for transfers between devices  37.6 us (34%)
  blocking collectives  26.6 us (24%)
  matrix products  17.4 us (16%)
  between operations  13.5 us (12%)
  other arithmetic  9.97 us (9%)
  local copies, waits for them, and re-layouts  6.75 us (6%)
    psum x1, waiting for transfers between devices, per_device(): in_factor, out_factor = lax.psum((input_part, output_part), 'proj')  27.2 us
    all_gather x1, blocking collectives, score_block(): lax.all_gather(queries, ('blk', 'rep'), axis=0, tiled=True)  16.5 us
    unnamed x3, waiting for transfers between devices  10.4 us
    all_to_all x1, blocking collectives, per_device(): lax.all_to_all(outgoing, 'blk', split_axis=1, concat_axis=1, tiled=True)  10.1 us
    dot_general x1, matrix products, per_device(): jnp.dot(activations, in_proj, preferred_element_type=jnp.float32)  7.65 us
    convert_element_type x1, other arithmetic, per_device(): token_grads = (input_local[:, :, None] * out_factor[:, None, :]).reshape(...  7.37 us
    dot_general x1, matrix products, score_block(): lax.dot_general(lax.all_gather(queries, ('blk', 'rep'), axis=0, tiled=Tru...  5.99 us
    dot_general x1, matrix products, per_device(): jnp.dot(out_grads, out_proj, preferred_element_type=jnp.float32)  3.78 us
  transfers between devices with their start and end apart: 2, of which 2 were waited for; matrix products, arithmetic and copies ran while one was open for 2% of the time, Pallas kernels for 0%

commit v1 on v0

v1 whole, which is shorter than its diff:
```python
import functools

import jax
import jax.numpy as jnp
from jax import lax
from jax.experimental import pallas as pl
from jax.experimental.pallas import tpu as pltpu
from jax.sharding import PartitionSpec as P

CAP = 64
F32 = jnp.float32
BF16 = jnp.bfloat16


def kernel(sizes, act, og, wi, wo, qin, counts, owners, out, abuf, gbuf, wraw, wpad, qbuf, sbuf,
           rbuf, dg, dgb, ft, scores, spack, rpack, load_a, load_g, load_w, load_q, fsend, frecv,
           a_send, a_recv, b_send, b_recv, c_send, c_recv, d_send, d_recv, s_send, s_recv):
    ny, nz, nx, nc, part, chunk = sizes
    steps = part // chunk
    x, y = lax.axis_index("proj"), lax.axis_index("groups")
    z, c = lax.axis_index("blk"), lax.axis_index("rep")
    ki, ko = wi.shape[1], wo.shape[1]
    width = qbuf.shape[-1]
    qrows = qin.shape[0]
    docs = counts.shape[1]
    columns = nz * CAP

    def put(src, dst, send, recv, **where):
        return pltpu.make_async_remote_copy(
            src_ref=src, dst_ref=dst, send_sem=send, recv_sem=recv,
            device_id=where, device_id_type=pl.DeviceIdType.MESH,
        )

    def at(index, step, n):
        return lax.rem(index + step, n)

    w_loads = [
        pltpu.make_async_copy(wi, wraw.at[0], load_w.at[0]),
        pltpu.make_async_copy(wo, wraw.at[1], load_w.at[1]),
    ]
    q_load = pltpu.make_async_copy(
        qin.at[:, pl.ds(pl.multiple_of(y * width, 128), width)], qbuf.at[y, c, x, z], load_q
    )
    q_load.start()
    w_loads[0].start()
    w_loads[1].start()
    order = [(dx % nx, i) for dx in range(1, nx + 1) for i in range(steps)]
    loads = []
    for n, (dx, i) in enumerate(order):
        first = pl.multiple_of(at(x, dx, nx) * part + i * chunk, 16)
        pair = (
            pltpu.make_async_copy(act.at[pl.ds(first, chunk), :], abuf.at[n], load_a.at[n]),
            pltpu.make_async_copy(og.at[pl.ds(first, chunk), :], gbuf.at[n], load_g.at[n]),
        )
        pair[0].start()
        pair[1].start()
        loads.append(pair)

    barrier = pltpu.get_barrier_semaphore()
    peers = [
        {"proj": at(x, dx, nx), "blk": at(z, dz, nz)}
        for dx in range(nx) for dz in range(nz) if dx or dz
    ]
    peers += [{"groups": at(y, dy, ny)} for dy in range(1, ny)]
    peers += [{"rep": at(c, dc, nc)} for dc in range(1, nc)]
    for peer in peers:
        pl.semaphore_signal(barrier, inc=1, device_id=peer, device_id_type=pl.DeviceIdType.MESH)

    lengths = counts[...].astype(F32)
    named = owners[...].astype(F32)
    row = lax.broadcasted_iota(jnp.int32, (docs, docs), 0)
    col = lax.broadcasted_iota(jnp.int32, (docs, docs), 1)
    starts = jnp.sum(jnp.where(col < row, lengths, 0.0), axis=1, keepdims=True)
    ends = jnp.sum(jnp.where(col <= row, lengths, 0.0), axis=1, keepdims=True)
    mine = jnp.sum(jnp.where(col == row, named, 0.0), axis=1, keepdims=True)
    rank = jnp.sum(
        jnp.where((col < row) & (named == mine), 1.0, 0.0), axis=1, keepdims=True
    )
    slot = (mine * CAP + rank).astype(jnp.int32)
    hit = slot == lax.broadcasted_iota(jnp.int32, (docs, columns), 1)
    col_start = jnp.sum(jnp.where(hit, starts, 0.0), axis=0, keepdims=True).astype(jnp.int32)
    col_end = jnp.sum(jnp.where(hit, ends, 0.0), axis=0, keepdims=True).astype(jnp.int32)

    for w in w_loads:
        w.wait()
    blank = jnp.zeros((wi.shape[0], ko), BF16)
    wpad[0] = jnp.concatenate([wraw[0], blank], axis=1)
    wpad[1] = jnp.concatenate([blank, wraw[1]], axis=1)
    q_load.wait()
    pl.semaphore_wait(barrier, len(peers))

    pending = []
    qa = {}
    qb = {}
    for dx in range(1, nx):
        qa[dx] = put(qbuf.at[y, c, x, z], qbuf.at[y, c, x, z], a_send.at[dx], a_recv.at[dx],
                     proj=at(x, dx, nx))
        qa[dx].start()

    def spread(j):
        from_x = at(x, nx - j, nx)
        for dz in range(1, nz):
            qb[j, dz] = put(qbuf.at[y, c, from_x, z], qbuf.at[y, c, from_x, z],
                            b_send.at[j, dz], b_recv.at[j, dz], blk=at(z, dz, nz))
            qb[j, dz].start()

    spread(0)

    def factors(n):
        loads[n][0].wait()
        loads[n][1].wait()
        return jnp.dot(abuf[n], wpad[0], preferred_element_type=F32) + jnp.dot(
            gbuf[n], wpad[1], preferred_element_type=F32
        )

    fx = {}
    for n, (dx, i) in enumerate(order):
        if dx == 0:
            break
        sbuf[dx - 1, i] = factors(n).astype(BF16)
        fx[dx, i] = put(sbuf.at[dx - 1, i], rbuf.at[dx - 1, i], fsend.at[dx - 1, i],
                        frecv.at[dx - 1, i], proj=at(x, dx, nx))
        fx[dx, i].start()
        if n == 0:
            for j in range(1, nx):
                qa[j].wait_recv()
                spread(j)

    yz = [
        put(qbuf.at[y, c], qbuf.at[y, c], c_send.at[dy], c_recv.at[dy], groups=at(y, dy, ny))
        for dy in range(1, ny)
    ]

    def to_cores(dy):
        from_y = at(y, ny - dy, ny)
        found = []
        for dc in range(1, nc):
            copy = put(qbuf.at[from_y, c], qbuf.at[from_y, c], d_send.at[dy, dc],
                       d_recv.at[dy, dc], rep=at(c, dc, nc))
            copy.start()
            found.append(copy)
        return found

    cores = []
    group = 8 * ko
    for i in range(steps):
        own = factors((nx - 1) * steps + i)
        if i == steps - 1:
            for copy in qb.values():
                copy.wait_recv()
            for copy in yz:
                copy.start()
            cores += to_cores(0)
        for dx in range(1, nx):
            fx[dx, i].wait_recv()
            own = own + rbuf[dx - 1, i].astype(F32)
        ft[...] = own.T
        position = x * part + i * chunk + lax.broadcasted_iota(jnp.int32, (chunk, columns), 0)
        member = jnp.where(
            (position >= col_start) & (position < col_end), 1.0, 0.0
        ).astype(BF16)

        def body(k, carry):
            out_t = ft[ki:ki + ko, :]
            in_t = ft[pl.ds(pl.multiple_of(k * 8, 8), 8), :]
            grads = jnp.concatenate(
                [(in_t[b:b + 1, :] * out_t).astype(BF16) for b in range(8)], axis=0
            )
            total = jnp.dot(grads, member, preferred_element_type=F32)
            rows = pl.ds(pl.multiple_of(k * group, group), group)
            if i > 0:
                total = total + dg[rows, :]
            if i < steps - 1:
                dg[rows, :] = total
            else:
                dgb[rows, :] = total.astype(BF16)
            return carry

        lax.fori_loop(0, ki // 8, body, 0)

    for dy in range(1, ny):
        yz[dy - 1].wait_recv()
        cores += to_cores(dy)
    for copy in cores:
        copy.wait_recv()

    total = None
    for xx in range(nx):
        for yy in range(ny):
            queries = jnp.concatenate(
                [qbuf[yy, cc, xx, zz] for cc in range(nc) for zz in range(nz)], axis=0
            )
            base = (xx * ny + yy) * width
            term = jnp.dot(queries, dgb[base:base + width, :], preferred_element_type=F32)
            total = term if total is None else total + term
    scores[...] = total

    per = nz // nx
    half = per * nc * qrows // 2
    low_lanes = lax.broadcasted_iota(jnp.int32, (half, 2 * CAP), 1) < CAP
    for xx in range(nx):
        starts_at = [
            (cc * nz + xx * per + zz) * qrows for zz in range(per) for cc in range(nc)
        ]
        for pair in range(nz // 2):
            lanes = slice(pair * 2 * CAP, (pair + 1) * 2 * CAP)
            block = jnp.concatenate([scores[s:s + qrows, lanes] for s in starts_at], axis=0)
            low, high = block[:half], block[half:]
            spack[2 * pair, xx] = jnp.where(low_lanes, low, pltpu.roll(high, CAP, 1))
            spack[2 * pair + 1, xx] = jnp.where(low_lanes, pltpu.roll(low, CAP, 1), high)
    sx = []
    for dx in range(nx):
        for dz in range(nz):
            if dx or dz:
                to_x, to_z = at(x, dx, nx), at(z, dz, nz)
                copy = put(spack.at[to_z, to_x], rpack.at[z, x], s_send.at[dx, dz],
                           s_recv.at[dx, dz], proj=to_x, blk=to_z)
                copy.start()
                sx.append(copy)
    rpack[z, x] = spack[z, x]
    for copy in sx:
        copy.wait_recv()
    for pair in range(nz // 2):
        lanes = slice(pair * 2 * CAP, (pair + 1) * 2 * CAP)
        left, right = rpack[2 * pair, 0], rpack[2 * pair + 1, 0]
        for xx in range(1, nx):
            left = left + rpack[2 * pair, xx]
            right = right + rpack[2 * pair + 1, xx]
        out[:half, lanes] = jnp.where(low_lanes, left, pltpu.roll(right, CAP, 1))
        out[half:, lanes] = jnp.where(low_lanes, pltpu.roll(left, CAP, 1), right)

    for copy in [*qa.values(), *qb.values(), *fx.values(), *yz, *cores, *sx]:
        copy.wait_send()


def per_device(sizes, activations, out_grads, in_proj, out_proj, precond_queries, counts, owners):
    ny, nz, nx, nc = sizes
    tokens, depth = activations.shape
    ki, ko = in_proj.shape[1], out_proj.shape[1]
    part = tokens // nx
    chunk = 384 if part % 384 == 0 else part
    steps = part // chunk
    count = nx * steps
    qrows, qcols = precond_queries.shape
    width = qcols // ny
    columns = nz * CAP
    feats = ki * ko
    queries = nz * nc * qrows
    rows = queries // nx
    dma = pltpu.SemaphoreType.DMA
    hbm = pl.BlockSpec(memory_space=pl.ANY)
    vmem = pl.BlockSpec(memory_space=pltpu.VMEM)
    others = max(nx - 1, 1)
    return pl.pallas_call(
        functools.partial(kernel, (*sizes, part, chunk)),
        out_shape=jax.ShapeDtypeStruct((rows, nz * CAP), F32),
        in_specs=[hbm] * 5 + [vmem] * 2,
        out_specs=vmem,
        scratch_shapes=[
            pltpu.VMEM((count, chunk, depth), BF16),
            pltpu.VMEM((count, chunk, depth), BF16),
            pltpu.VMEM((2, depth, ki), BF16),
            pltpu.VMEM((2, depth, ki + ko), BF16),
            pltpu.VMEM((ny, nc, nx, nz, qrows, width), BF16),
            pltpu.VMEM((others, steps, chunk, ki + ko), BF16),
            pltpu.VMEM((others, steps, chunk, ki + ko), BF16),
            pltpu.VMEM((feats, columns) if steps > 1 else (8, 128), F32),
            pltpu.VMEM((feats, columns), BF16),
            pltpu.VMEM((ki + ko, chunk), F32),
            pltpu.VMEM((queries, columns), F32),
            pltpu.VMEM((nz, nx, rows // 2, 2 * CAP), F32),
            pltpu.VMEM((nz, nx, rows // 2, 2 * CAP), F32),
            dma((count,)),
            dma((count,)),
            dma((2,)),
            dma,
            dma((others, steps)),
            dma((others, steps)),
            dma((nx,)),
            dma((nx,)),
            dma((nx, nz)),
            dma((nx, nz)),
            dma((ny,)),
            dma((ny,)),
            dma((ny, nc)),
            dma((ny, nc)),
            dma((nx, nz)),
            dma((nx, nz)),
        ],
        compiler_params=pltpu.CompilerParams(
            collective_id=0, has_side_effects=True, vmem_limit_bytes=56 * 1024 * 1024
        ),
        cost_estimate=pl.CostEstimate(
            flops=4 * tokens * depth * ki + 2 * part * feats * columns,
            bytes_accessed=4 * tokens * depth,
            transcendentals=0,
        ),
    )(activations, out_grads, in_proj, out_proj, precond_queries, counts, owners)


def solution(mesh):
    placed = (
        P(("groups", "blk", "rep"), "proj"),
        P(("groups", "blk", "rep"), "proj"),
        P("proj", None),
        P("proj", None),
        P(("blk", "rep"), "proj"),
        P(("groups", "blk", "rep"), None),
        P(("groups", "blk", "rep"), None),
    )
    sizes = tuple(mesh.shape[name] for name in ("groups", "blk", "proj", "rep"))
    return jax.shard_map(
        functools.partial(per_device, sizes),
        mesh=mesh,
        in_specs=placed,
        out_specs=P("proj", ("groups", "blk", "rep")),
        check_vma=False,
    )
```

time: 112 us -> 45.9 us (0.41)
  Pallas kernels: 0 us -> 39.8 us
  waiting for transfers between devices: 37.6 us -> 0 us
  blocking collectives: 26.6 us -> 0 us
  matrix products: 17.4 us -> 0 us
  between operations: 13.5 us -> 0.01 us
  other arithmetic: 9.97 us -> 0 us
  local copies, waits for them, and re-layouts: 6.75 us -> 5.39 us
    pallas_call x0 -> x1, Pallas kernels: none -> 39.8 us  [per_device(): pl.pallas_call(functools.partial(kernel, (*sizes, part, chunk)), out_shap...]
    psum x1 -> x0, waiting for transfers between devices: 27.2 us -> none  [per_device(): in_factor, out_factor = lax.psum((input_part, output_part), 'proj')]
    dot_general x3 -> x0, matrix products: 17.4 us -> none  [the longest x1 7.65 us: per_device(): jnp.dot(activations, in_proj, preferred_element_type=jnp.float32)]
    all_gather x1 -> x0, blocking collectives: 16.5 us -> none  [score_block(): lax.all_gather(queries, ('blk', 'rep'), axis=0, tiled=True)]
    unnamed x3 -> x0, waiting for transfers between devices: 10.4 us -> none
    all_to_all x1 -> x0, blocking collectives: 10.1 us -> none  [per_device(): lax.all_to_all(outgoing, 'blk', split_axis=1, concat_axis=1, tiled=True)]
    convert_element_type x2 -> x0, other arithmetic: 7.38 us -> none  [the longest x1 7.37 us: per_device(): token_grads = (input_local[:, :, None] * out_factor[:, None, :]).reshape(...]
    unnamed x16 -> x3, local copies, waits for them, and re-layouts: 2.88 us -> 5.39 us
  transfers between devices with their start and end apart: 2 -> 0, of which waited for: 2 -> 0; matrix products, arithmetic and copies ran while one was open for 2% -> 0% of each run, Pallas kernels for 0% -> 0%
where the time goes in v1:
time: 45.9 us; the launch traced here: 45.2 us
  Pallas kernels  39.8 us (87%)
  local copies, waits for them, and re-layouts  5.39 us (12%)
    pallas_call x1, Pallas kernels, per_device(): pl.pallas_call(functools.partial(kernel, (*sizes, part, chunk)), out_shap...  39.8 us
    unnamed x3, local copies, waits for them, and re-layouts  5.39 us

profile of v1, /device:TPU:0, one launch (start us, length us, event | category | flops | bytes accessed | tf_op | source)
XLA Modules:
  0.0 45.2 jit_solution(16155744300094588566)
XLA Ops:
  0.0 1.9 %copy.8.wi = bf16[2048,64]{1,0:T(8,128)(2,1)} copy(bf16[2048,64]{0,1:T(8,128)(2,1)} %param.9) | data formatting | bytes 524288 | tf_op args[2]
  1.9 2.0 %copy.9.wo = bf16[2048,64]{1,0:T(8,128)(2,1)} copy(bf16[2048,64]{0,1:T(8,128)(2,1)} %param.10) | data formatting | bytes 524288 | tf_op args[3]
  3.9 39.8 %shard_map.73 = f32[64,256]{1,0:T(8,128)} custom-call(bf16[2304,2048]{1,0:T(8,128)(2,1)} %act.1, bf16[2304,2048]{1,0:T(8,128)(2,1)} %og.1, bf16[2048,64]{1,0:T(8,128)(2,1)} %copy.8.wi, bf16[2048,64]{1,0:T(8,128)(2,1)} %copy.9.wo, bf16[16,2048]{1,0:T(8,128)(2,1)} %qin.1, s32[1,256]{1,0:T(1,128)} %counts.1, s32[1,256]{1,0:T(1,128)} %owners.1), custom_call_target="tpu_custom_call" | custom-call | flops 3623878656 | bytes 18874368 | tf_op jit(solution)/shard_map/pallas_call | solution.py:254
  43.8 1.5 %copy.11 = f32[64,256]{1,0:T(8,128)} copy(f32[64,256]{1,0:T(8,128)} %shard_map.73) | data formatting | bytes 131072

commit v2 on v1

--- a/solution.py
+++ b/solution.py
@@ -13,13 +13,13 @@
 
 
 def kernel(sizes, act, og, wi, wo, qin, counts, owners, out, abuf, gbuf, wraw, wpad, qbuf, sbuf,
-           rbuf, dg, dgb, ft, scores, spack, rpack, load_a, load_g, load_w, load_q, fsend, frecv,
-           a_send, a_recv, b_send, b_recv, c_send, c_recv, d_send, d_recv, s_send, s_recv):
-    ny, nz, nx, nc, part, chunk = sizes
-    steps = part // chunk
+           rbuf, own, dg, dgb, ft, scores, spack, rpack, load_a, load_g, load_w, load_q, fsend,
+           frecv, a_send, a_recv, b_send, b_recv, c_send, c_recv, d_send, d_recv, s_send, s_recv):
+    ny, nz, nx, nc, part, chunks = sizes
+    steps = len(chunks)
     x, y = lax.axis_index("proj"), lax.axis_index("groups")
     z, c = lax.axis_index("blk"), lax.axis_index("rep")
-    ki, ko = wi.shape[1], wo.shape[1]
+    ki, ko = wi.shape[0], wo.shape[0]
     width = qbuf.shape[-1]
     qrows = qin.shape[0]
     docs = counts.shape[1]
@@ -34,23 +34,31 @@
     def at(index, step, n):
         return lax.rem(index + step, n)
 
+    q_loads = [
+        pltpu.make_async_copy(
+            qin.at[:, yy * width:(yy + 1) * width], qbuf.at[yy, c, x, z], load_q.at[yy]
+        )
+        for yy in range(ny)
+    ]
     w_loads = [
         pltpu.make_async_copy(wi, wraw.at[0], load_w.at[0]),
         pltpu.make_async_copy(wo, wraw.at[1], load_w.at[1]),
     ]
-    q_load = pltpu.make_async_copy(
-        qin.at[:, pl.ds(pl.multiple_of(y * width, 128), width)], qbuf.at[y, c, x, z], load_q
-    )
-    q_load.start()
-    w_loads[0].start()
-    w_loads[1].start()
+    for copy in [*w_loads, *q_loads]:
+        copy.start()
     order = [(dx % nx, i) for dx in range(1, nx + 1) for i in range(steps)]
     loads = []
     for n, (dx, i) in enumerate(order):
-        first = pl.multiple_of(at(x, dx, nx) * part + i * chunk, 16)
+        offset, size = chunks[i]
+        first = pl.multiple_of(at(x, dx, nx) * part + offset, 16)
+        rows = pl.ds(offset, size)
         pair = (
-            pltpu.make_async_copy(act.at[pl.ds(first, chunk), :], abuf.at[n], load_a.at[n]),
-            pltpu.make_async_copy(og.at[pl.ds(first, chunk), :], gbuf.at[n], load_g.at[n]),
+            pltpu.make_async_copy(
+                act.at[pl.ds(first, size), :], abuf.at[dx, rows, :], load_a.at[n]
+            ),
+            pltpu.make_async_copy(
+                og.at[pl.ds(first, size), :], gbuf.at[dx, rows, :], load_g.at[n]
+            ),
         )
         pair[0].start()
         pair[1].start()
@@ -83,106 +91,142 @@
 
     for w in w_loads:
         w.wait()
-    blank = jnp.zeros((wi.shape[0], ko), BF16)
-    wpad[0] = jnp.concatenate([wraw[0], blank], axis=1)
-    wpad[1] = jnp.concatenate([blank, wraw[1]], axis=1)
-    q_load.wait()
-    pl.semaphore_wait(barrier, len(peers))
-
-    pending = []
-    qa = {}
-    qb = {}
-    for dx in range(1, nx):
-        qa[dx] = put(qbuf.at[y, c, x, z], qbuf.at[y, c, x, z], a_send.at[dx], a_recv.at[dx],
-                     proj=at(x, dx, nx))
-        qa[dx].start()
-
-    def spread(j):
-        from_x = at(x, nx - j, nx)
-        for dz in range(1, nz):
-            qb[j, dz] = put(qbuf.at[y, c, from_x, z], qbuf.at[y, c, from_x, z],
-                            b_send.at[j, dz], b_recv.at[j, dz], blk=at(z, dz, nz))
-            qb[j, dz].start()
-
-    spread(0)
+    blank = jnp.zeros((ki, wi.shape[1]), BF16)
+    wpad[0] = jnp.concatenate([wraw[0], blank], axis=0).T
+    wpad[1] = jnp.concatenate([blank, wraw[1]], axis=0).T
 
     def factors(n):
+        dx, i = order[n]
+        offset, size = chunks[i]
         loads[n][0].wait()
         loads[n][1].wait()
-        return jnp.dot(abuf[n], wpad[0], preferred_element_type=F32) + jnp.dot(
-            gbuf[n], wpad[1], preferred_element_type=F32
+        rows = slice(offset, offset + size)
+        return jnp.dot(abuf[dx, rows, :], wpad[0], preferred_element_type=F32) + jnp.dot(
+            gbuf[dx, rows, :], wpad[1], preferred_element_type=F32
         )
 
+    sent = []
+    got = {}
+
+    def piece(yy, j, dz):
+        return qbuf.at[yy, c, at(x, nx - j, nx), at(z, nz - dz, nz)]
+
+    def go(key, copy):
+        copy.start()
+        sent.append(copy)
+        got[key] = copy
+
+    def along_z(j):
+        for dz in [1, *range(nz - 1, 1, -1)]:
+            ref = piece(y, j, 0)
+            go(("z", j, dz),
+               put(ref, ref, b_send.at[j, dz], b_recv.at[j, dz], blk=at(z, dz, nz)))
+
+    def along_y(j, dz):
+        for dy in range(1, ny):
+            ref = piece(y, j, dz)
+            go(("y", dy, j, dz),
+               put(ref, ref, c_send.at[dy, j, dz], c_recv.at[dy, j, dz], groups=at(y, dy, ny)))
+
+    def to_core(dy, j, dz):
+        for dc in range(1, nc):
+            ref = piece(at(y, ny - dy, ny), j, dz)
+            go(("c", dc, dy, j, dz),
+               put(ref, ref, d_send.at[dy, dc, j, dz], d_recv.at[dy, dc, j, dz],
+                   rep=at(c, dc, nc)))
+
+    def from_z(dz):
+        for j in range(nx):
+            got["z", j, dz].wait_recv()
+            along_y(j, dz)
+            to_core(0, j, dz)
+
+    def from_y(keys):
+        for dy in range(1, ny):
+            for j, dz in keys:
+                got["y", dy, j, dz].wait_recv()
+                to_core(dy, j, dz)
+
+    def begin():
+        for copy in q_loads:
+            copy.wait()
+        pl.semaphore_wait(barrier, len(peers))
+        for dx in range(1, nx):
+            ref = piece(y, 0, 0)
+            go(("x", dx), put(ref, ref, a_send.at[dx], a_recv.at[dx], proj=at(x, dx, nx)))
+        along_z(0)
+
     fx = {}
+    if nx == 1:
+        begin()
     for n, (dx, i) in enumerate(order):
+        offset, size = chunks[i]
+        rows = slice(offset, offset + size)
         if dx == 0:
-            break
-        sbuf[dx - 1, i] = factors(n).astype(BF16)
-        fx[dx, i] = put(sbuf.at[dx - 1, i], rbuf.at[dx - 1, i], fsend.at[dx - 1, i],
-                        frecv.at[dx - 1, i], proj=at(x, dx, nx))
+            own[rows, :] = factors(n)
+            if i == 0:
+                for j in range(1, nx):
+                    got["x", j].wait_recv()
+                    along_z(j)
+                    along_y(j, 0)
+                    to_core(0, j, 0)
+                for dy in range(ny):
+                    to_core(dy, 0, 0)
+            continue
+        sbuf[dx - 1, rows, :] = factors(n).astype(BF16)
+        if n == 0:
+            begin()
+        part_rows = pl.ds(offset, size)
+        fx[dx, i] = put(sbuf.at[dx - 1, part_rows, :], rbuf.at[dx - 1, part_rows, :],
+                        fsend.at[dx - 1, i], frecv.at[dx - 1, i], proj=at(x, dx, nx))
         fx[dx, i].start()
-        if n == 0:
-            for j in range(1, nx):
-                qa[j].wait_recv()
-                spread(j)
-
-    yz = [
-        put(qbuf.at[y, c], qbuf.at[y, c], c_send.at[dy], c_recv.at[dy], groups=at(y, dy, ny))
-        for dy in range(1, ny)
-    ]
-
-    def to_cores(dy):
-        from_y = at(y, ny - dy, ny)
-        found = []
-        for dc in range(1, nc):
-            copy = put(qbuf.at[from_y, c], qbuf.at[from_y, c], d_send.at[dy, dc],
-                       d_recv.at[dy, dc], rep=at(c, dc, nc))
-            copy.start()
-            found.append(copy)
-        return found
-
-    cores = []
-    group = 8 * ko
-    for i in range(steps):
-        own = factors((nx - 1) * steps + i)
+
+    near = [1, nz - 1] if nz > 2 else [1]
+    far = [dz for dz in range(1, nz) if dz not in near]
+    block = 32
+    group = block * ko
+    for i, (offset, size) in enumerate(chunks):
+        rows = slice(offset, offset + size)
+        if i == 0:
+            from_z(near[0])
+        if i == min(1, steps - 1):
+            for dz in near[1:] + far:
+                from_z(dz)
         if i == steps - 1:
-            for copy in qb.values():
-                copy.wait_recv()
-            for copy in yz:
-                copy.start()
-            cores += to_cores(0)
+            from_y([(j, 0) for j in range(1, nx)])
+            for dz in near + far:
+                from_y([(j, dz) for j in range(nx)])
+        here = own[rows, :]
         for dx in range(1, nx):
             fx[dx, i].wait_recv()
-            own = own + rbuf[dx - 1, i].astype(F32)
-        ft[...] = own.T
-        position = x * part + i * chunk + lax.broadcasted_iota(jnp.int32, (chunk, columns), 0)
+            here = here + rbuf[dx - 1, rows, :].astype(F32)
+        ft[:, :size] = here.T
+        position = x * part + offset + lax.broadcasted_iota(jnp.int32, (size, columns), 0)
         member = jnp.where(
             (position >= col_start) & (position < col_end), 1.0, 0.0
         ).astype(BF16)
 
         def body(k, carry):
-            out_t = ft[ki:ki + ko, :]
-            in_t = ft[pl.ds(pl.multiple_of(k * 8, 8), 8), :]
+            out_t = ft[ki:ki + ko, :size]
+            in_t = ft[pl.ds(pl.multiple_of(k * block, block), block), :size]
             grads = jnp.concatenate(
-                [(in_t[b:b + 1, :] * out_t).astype(BF16) for b in range(8)], axis=0
+                [(in_t[b:b + 1, :] * out_t).astype(BF16) for b in range(block)], axis=0
             )
             total = jnp.dot(grads, member, preferred_element_type=F32)
-            rows = pl.ds(pl.multiple_of(k * group, group), group)
+            places = pl.ds(pl.multiple_of(k * group, group), group)
             if i > 0:
-                total = total + dg[rows, :]
+                total = total + dg[places, :]
             if i < steps - 1:
-                dg[rows, :] = total
+                dg[places, :] = total
             else:
-                dgb[rows, :] = total.astype(BF16)
+                dgb[places, :] = total.astype(BF16)
             return carry
 
-        lax.fori_loop(0, ki // 8, body, 0)
-
-    for dy in range(1, ny):
-        yz[dy - 1].wait_recv()
-        cores += to_cores(dy)
-    for copy in cores:
-        copy.wait_recv()
+        lax.fori_loop(0, ki // block, body, 0)
+
+    for key, copy in got.items():
+        if key[0] == "c":
+            copy.wait_recv()
 
     total = None
     for xx in range(nx):
@@ -229,7 +273,7 @@
         out[:half, lanes] = jnp.where(low_lanes, left, pltpu.roll(right, CAP, 1))
         out[half:, lanes] = jnp.where(low_lanes, pltpu.roll(left, CAP, 1), right)
 
-    for copy in [*qa.values(), *qb.values(), *fx.values(), *yz, *cores, *sx]:
+    for copy in [*sent, *fx.values(), *sx]:
         copy.wait_send()
 
 
@@ -238,8 +282,8 @@
     tokens, depth = activations.shape
     ki, ko = in_proj.shape[1], out_proj.shape[1]
     part = tokens // nx
-    chunk = 384 if part % 384 == 0 else part
-    steps = part // chunk
+    chunks = tuple((first, min(512, part - first)) for first in range(0, part, 512))
+    steps = len(chunks)
     count = nx * steps
     qrows, qcols = precond_queries.shape
     width = qcols // ny
@@ -252,38 +296,39 @@
     vmem = pl.BlockSpec(memory_space=pltpu.VMEM)
     others = max(nx - 1, 1)
     return pl.pallas_call(
-        functools.partial(kernel, (*sizes, part, chunk)),
+        functools.partial(kernel, (*sizes, part, chunks)),
         out_shape=jax.ShapeDtypeStruct((rows, nz * CAP), F32),
         in_specs=[hbm] * 5 + [vmem] * 2,
         out_specs=vmem,
         scratch_shapes=[
-            pltpu.VMEM((count, chunk, depth), BF16),
-            pltpu.VMEM((count, chunk, depth), BF16),
-            pltpu.VMEM((2, depth, ki), BF16),
+            pltpu.VMEM((nx, part, depth), BF16),
+            pltpu.VMEM((nx, part, depth), BF16),
+            pltpu.VMEM((2, ki, depth), BF16),
             pltpu.VMEM((2, depth, ki + ko), BF16),
             pltpu.VMEM((ny, nc, nx, nz, qrows, width), BF16),
-            pltpu.VMEM((others, steps, chunk, ki + ko), BF16),
-            pltpu.VMEM((others, steps, chunk, ki + ko), BF16),
+            pltpu.VMEM((others, part, ki + ko), BF16),
+            pltpu.VMEM((others, part, ki + ko), BF16),
+            pltpu.VMEM((part, ki + ko), F32),
             pltpu.VMEM((feats, columns) if steps > 1 else (8, 128), F32),
             pltpu.VMEM((feats, columns), BF16),
-            pltpu.VMEM((ki + ko, chunk), F32),
+            pltpu.VMEM((ki + ko, chunks[0][1]), F32),
             pltpu.VMEM((queries, columns), F32),
             pltpu.VMEM((nz, nx, rows // 2, 2 * CAP), F32),
             pltpu.VMEM((nz, nx, rows // 2, 2 * CAP), F32),
             dma((count,)),
             dma((count,)),
             dma((2,)),
-            dma,
+            dma((ny,)),
             dma((others, steps)),
             dma((others, steps)),
             dma((nx,)),
             dma((nx,)),
             dma((nx, nz)),
             dma((nx, nz)),
-            dma((ny,)),
-            dma((ny,)),
-            dma((ny, nc)),
-            dma((ny, nc)),
+            dma((ny, nx, nz)),
+            dma((ny, nx, nz)),
+            dma((ny, nc, nx, nz)),
+            dma((ny, nc, nx, nz)),
             dma((nx, nz)),
             dma((nx, nz)),
         ],
@@ -295,7 +340,7 @@
             bytes_accessed=4 * tokens * depth,
             transcendentals=0,
         ),
-    )(activations, out_grads, in_proj, out_proj, precond_queries, counts, owners)
+    )(activations, out_grads, in_proj.T, out_proj.T, precond_queries, counts, owners)
 
 
 def solution(mesh):

time: 45.9 us -> 36.6 us (0.80); the launches traced: 45.2 us -> 36.4 us
  Pallas kernels: 39.8 us -> 34.9 us
  local copies, waits for them, and re-layouts: 5.39 us -> 1.47 us
    pallas_call x1, Pallas kernels: 39.8 us -> 34.9 us  [per_device(): pl.pallas_call(functools.partial(kernel, (*sizes, part, chunks)), out_sha...]
    unnamed x3 -> x1, local copies, waits for them, and re-layouts: 5.39 us -> 1.47 us
where the time goes in v2:
time: 36.6 us; the launch traced here: 36.4 us
  Pallas kernels  34.9 us (95%)
  local copies, waits for them, and re-layouts  1.47 us (4%)
    pallas_call x1, Pallas kernels, per_device(): pl.pallas_call(functools.partial(kernel, (*sizes, part, chunks)), out_sha...  34.9 us
    unnamed x1, local copies, waits for them, and re-layouts  1.47 us

profile of v2, /device:TPU:0, one launch (start us, length us, event | category | flops | bytes accessed | tf_op | source)
XLA Modules:
  0.0 36.4 jit_solution(12588504111072837923)
XLA Ops:
  0.0 34.9 %shard_map.73 = f32[64,256]{1,0:T(8,128)} custom-call(bf16[2304,2048]{1,0:T(8,128)(2,1)} %act.1, bf16[2304,2048]{1,0:T(8,128)(2,1)} %og.1, bf16[64,2048]{1,0:T(8,128)(2,1)} %bitcast.2, bf16[64,2048]{1,0:T(8,128)(2,1)} %bitcast.3, bf16[16,2048]{1,0:T(8,128)(2,1)} %qin.1, s32[1,256]{1,0:T(1,128)} %counts.1, s32[1,256]{1,0:T(1,128)} %owners.1), custom_call_target="tpu_custom_call" | custom-call | flops 3623878656 | bytes 18874368 | tf_op jit(solution)/shard_map/pallas_call | solution.py:298
  34.9 1.5 %copy.9 = f32[64,256]{1,0:T(8,128)} copy(f32[64,256]{1,0:T(8,128)} %shard_map.73) | data formatting | bytes 131072

commit v3 on v2

--- a/solution.py
+++ b/solution.py
@@ -8,12 +8,14 @@
 from jax.sharding import PartitionSpec as P
 
 CAP = 64
+CHUNK = 384
+GROUP = 4
 F32 = jnp.float32
 BF16 = jnp.bfloat16
 
 
 def kernel(sizes, act, og, wi, wo, qin, counts, owners, out, abuf, gbuf, wraw, wpad, qbuf, sbuf,
-           rbuf, own, dg, dgb, ft, scores, spack, rpack, load_a, load_g, load_w, load_q, fsend,
+           rbuf, own, dgb, ft, scores, spack, rpack, load_a, load_g, load_w, load_q, fsend,
            frecv, a_send, a_recv, b_send, b_recv, c_send, c_recv, d_send, d_recv, s_send, s_recv):
     ny, nz, nx, nc, part, chunks = sizes
     steps = len(chunks)
@@ -60,8 +62,8 @@
                 og.at[pl.ds(first, size), :], gbuf.at[dx, rows, :], load_g.at[n]
             ),
         )
-        pair[0].start()
-        pair[1].start()
+        pair[0].start(priority=1)
+        pair[1].start(priority=1)
         loads.append(pair)
 
     barrier = pltpu.get_barrier_semaphore()
@@ -164,65 +166,56 @@
         rows = slice(offset, offset + size)
         if dx == 0:
             own[rows, :] = factors(n)
-            if i == 0:
-                for j in range(1, nx):
-                    got["x", j].wait_recv()
-                    along_z(j)
-                    along_y(j, 0)
-                    to_core(0, j, 0)
-                for dy in range(ny):
-                    to_core(dy, 0, 0)
             continue
         sbuf[dx - 1, rows, :] = factors(n).astype(BF16)
         if n == 0:
             begin()
-        part_rows = pl.ds(offset, size)
-        fx[dx, i] = put(sbuf.at[dx - 1, part_rows, :], rbuf.at[dx - 1, part_rows, :],
-                        fsend.at[dx - 1, i], frecv.at[dx - 1, i], proj=at(x, dx, nx))
-        fx[dx, i].start()
+        if n == len(order) - steps - 1:
+            for j in range(1, nx):
+                got["x", j].wait_recv()
+                along_z(j)
+                along_y(j, 0)
+                to_core(0, j, 0)
+            for dy in range(ny):
+                to_core(dy, 0, 0)
+            for to_x, k in order[:n + 1]:
+                held = pl.ds(*chunks[k])
+                fx[to_x, k] = put(
+                    sbuf.at[to_x - 1, held, :], rbuf.at[to_x - 1, held, :],
+                    fsend.at[to_x - 1, k], frecv.at[to_x - 1, k], proj=at(x, to_x, nx))
+                fx[to_x, k].start()
 
     near = [1, nz - 1] if nz > 2 else [1]
     far = [dz for dz in range(1, nz) if dz not in near]
-    block = 32
-    group = block * ko
+    from_z(near[0])
     for i, (offset, size) in enumerate(chunks):
         rows = slice(offset, offset + size)
-        if i == 0:
-            from_z(near[0])
-        if i == min(1, steps - 1):
-            for dz in near[1:] + far:
-                from_z(dz)
-        if i == steps - 1:
-            from_y([(j, 0) for j in range(1, nx)])
-            for dz in near + far:
-                from_y([(j, dz) for j in range(nx)])
         here = own[rows, :]
         for dx in range(1, nx):
             fx[dx, i].wait_recv()
             here = here + rbuf[dx - 1, rows, :].astype(F32)
-        ft[:, :size] = here.T
-        position = x * part + offset + lax.broadcasted_iota(jnp.int32, (size, columns), 0)
-        member = jnp.where(
-            (position >= col_start) & (position < col_end), 1.0, 0.0
+        ft[:, rows] = here.T
+        if i == 0:
+            for dz in near[1:] + far:
+                from_z(dz)
+    from_y([(j, 0) for j in range(1, nx)])
+    for dz in near:
+        from_y([(j, dz) for j in range(nx)])
+    position = x * part + lax.broadcasted_iota(jnp.int32, (part, columns), 0)
+    member = jnp.where(
+        (position >= col_start) & (position < col_end), 1.0, 0.0
+    ).astype(BF16)
+    for first in range(0, ki, GROUP):
+        if first == ki // 2:
+            for dz in far:
+                from_y([(j, dz) for j in range(nx)])
+        out_t = ft[ki:, :]
+        grads = jnp.concatenate(
+            [(ft[b:b + 1, :] * out_t).astype(BF16) for b in range(first, first + GROUP)], axis=0
+        )
+        dgb[first * ko:(first + GROUP) * ko, :] = jnp.dot(
+            grads, member, preferred_element_type=F32
         ).astype(BF16)
-
-        def body(k, carry):
-            out_t = ft[ki:ki + ko, :size]
-            in_t = ft[pl.ds(pl.multiple_of(k * block, block), block), :size]
-            grads = jnp.concatenate(
-                [(in_t[b:b + 1, :] * out_t).astype(BF16) for b in range(block)], axis=0
-            )
-            total = jnp.dot(grads, member, preferred_element_type=F32)
-            places = pl.ds(pl.multiple_of(k * group, group), group)
-            if i > 0:
-                total = total + dg[places, :]
-            if i < steps - 1:
-                dg[places, :] = total
-            else:
-                dgb[places, :] = total.astype(BF16)
-            return carry
-
-        lax.fori_loop(0, ki // block, body, 0)
 
     for key, copy in got.items():
         if key[0] == "c":
@@ -282,7 +275,7 @@
     tokens, depth = activations.shape
     ki, ko = in_proj.shape[1], out_proj.shape[1]
     part = tokens // nx
-    chunks = tuple((first, min(512, part - first)) for first in range(0, part, 512))
+    chunks = tuple((first, min(CHUNK, part - first)) for first in range(0, part, CHUNK))
     steps = len(chunks)
     count = nx * steps
     qrows, qcols = precond_queries.shape
@@ -309,9 +302,8 @@
             pltpu.VMEM((others, part, ki + ko), BF16),
             pltpu.VMEM((others, part, ki + ko), BF16),
             pltpu.VMEM((part, ki + ko), F32),
-            pltpu.VMEM((feats, columns) if steps > 1 else (8, 128), F32),
             pltpu.VMEM((feats, columns), BF16),
-            pltpu.VMEM((ki + ko, chunks[0][1]), F32),
+            pltpu.VMEM((ki + ko, part), F32),
             pltpu.VMEM((queries, columns), F32),
             pltpu.VMEM((nz, nx, rows // 2, 2 * CAP), F32),
             pltpu.VMEM((nz, nx, rows // 2, 2 * CAP), F32),

time: 36.6 us -> 33.4 us (0.913)
  Pallas kernels: 34.9 us -> 31.7 us
    pallas_call x1, Pallas kernels: 34.9 us -> 31.7 us  [per_device(): pl.pallas_call(functools.partial(kernel, (*sizes, part, chunks)), out_sha...]
where the time goes in v3:
time: 33.4 us; the launch traced here: 33.2 us
  Pallas kernels  31.7 us (95%)
  local copies, waits for them, and re-layouts  1.47 us (4%)
    pallas_call x1, Pallas kernels, per_device(): pl.pallas_call(functools.partial(kernel, (*sizes, part, chunks)), out_sha...  31.7 us
    unnamed x1, local copies, waits for them, and re-layouts  1.47 us

profile of v3, /device:TPU:0, one launch (start us, length us, event | category | flops | bytes accessed | tf_op | source)
XLA Modules:
  0.0 33.2 jit_solution(12460781724516979039)
XLA Ops:
  0.0 31.7 %shard_map.73 = f32[64,256]{1,0:T(8,128)} custom-call(bf16[2304,2048]{1,0:T(8,128)(2,1)} %act.1, bf16[2304,2048]{1,0:T(8,128)(2,1)} %og.1, bf16[64,2048]{1,0:T(8,128)(2,1)} %bitcast.2, bf16[64,2048]{1,0:T(8,128)(2,1)} %bitcast.3, bf16[16,2048]{1,0:T(8,128)(2,1)} %qin.1, s32[1,256]{1,0:T(1,128)} %counts.1, s32[1,256]{1,0:T(1,128)} %owners.1), custom_call_target="tpu_custom_call" | custom-call | flops 3623878656 | bytes 18874368 | tf_op jit(solution)/shard_map/pallas_call | solution.py:291
  31.7 1.5 %copy.9 = f32[64,256]{1,0:T(8,128)} copy(f32[64,256]{1,0:T(8,128)} %shard_map.73) | data formatting | bytes 131072
